TPU v7x, 32 devices: a whole 2x2x4 slice. The times are simulated.
32 devices in a mesh: expert: 8 (over y, x, core), dp: 4 (over z).
Axes of the slice: x: 2, y: 2, z: 4, core: 2. Of those that a mesh axis runs over, the one named last changes fastest.
Arguments:
- tokens: bfloat16 [512, 1664], P(('expert', 'dp')), may hold values from -6 to 6
- cotangent: bfloat16 [512, 1664], P(('expert', 'dp')), may hold values from -1.1953125 to 1.1953125
- expert_ids: int32 [512, 2], P(('expert', 'dp')), may hold values from 0 to 7, all different within a row; in each aligned block of 16 rows (0 to 15, 16 to 31, ...) at most 8 rows name the same one
- gates: bfloat16 [512, 2], P(('expert', 'dp')), may hold values from 0.099609375 to 1
- w_in: bfloat16 [8, 1664, 4096], P('expert', None, 'dp'), may hold values from -0.15625 to 0.15625
- w_out: bfloat16 [8, 4096, 1664], P('expert', 'dp'), may hold values from -0.09375 to 0.09375
Outputs:
- token_grads: bfloat16 [512, 1664], P(('expert', 'dp'))
- gate_grads: bfloat16 [512, 2], P(('expert', 'dp'))
- grad_in_weights: bfloat16 [8, 1664, 4096], P('expert', None, 'dp')
- grad_out_weights: bfloat16 [8, 4096, 1664], P('expert', 'dp')
Inputs may be any that keep to these rules, and one draw needn't show every extreme that they name: `expert_ids`: the two experts of a token differ, and no expert is named by more than 8 of the 16 tokens of one device.
All inputs are finite; a program needn't handle non-finite values.
Results may differ from a plain program's by a relative error of at most 0.019.
Values may be sent and summed in bfloat16 or wider, within the bound.
A program may use at most 64 MiB of HBM per device.

v0:
```python
import jax
import jax.numpy as jnp
from jax import lax
from jax.sharding import PartitionSpec as P


def normal_parts(pre):
    cdf = 0.5 * (1.0 + lax.erf(pre * 0.7071067811865476))
    pdf = 0.3989422804014327 * jnp.exp(-0.5 * pre * pre)
    return (cdf, pdf)


def per_device(tokens, cotangent, expert_ids, gates, w_in, w_out):
    tok = tokens.shape[0]
    feat = tokens.shape[1]
    experts = lax.axis_size("expert")
    cap = max(2, 4 * tok // experts)
    assign = 2 * tok
    ids = expert_ids.reshape(assign)
    onehot = (ids[:, None] == jnp.arange(experts, dtype=jnp.int32)[None, :]).astype(jnp.float32)
    lower = (jnp.arange(assign)[:, None] > jnp.arange(assign)[None, :]).astype(jnp.float32)
    before = jnp.dot(lower, onehot, preferred_element_type=jnp.float32)
    slot = jnp.sum(before * onehot, axis=1).astype(jnp.int32)
    target = ids * cap + slot
    pick = (jnp.arange(experts * cap, dtype=jnp.int32)[:, None] == target[None, :]).astype(
        jnp.bfloat16
    )
    src_in = jnp.repeat(tokens, 2, axis=0)
    src_cot = jnp.repeat(cotangent, 2, axis=0)
    send_in = (
        jnp.dot(pick, src_in, preferred_element_type=jnp.float32)
        .astype(jnp.bfloat16)
        .reshape(experts, cap, feat)
    )
    send_cot = (
        jnp.dot(pick, src_cot, preferred_element_type=jnp.float32)
        .astype(jnp.bfloat16)
        .reshape(experts, cap, feat)
    )
    send_gate = (
        jnp.dot(pick, gates.reshape(assign, 1), preferred_element_type=jnp.float32)
        .astype(jnp.bfloat16)
        .reshape(experts, cap)
    )
    w_first = w_in[0]
    w_second = w_out[0]
    arrived = (
        lax.all_to_all(send_in, "expert", split_axis=0, concat_axis=0, tiled=True),
        lax.all_to_all(send_cot, "expert", split_axis=0, concat_axis=0, tiled=True),
        lax.all_to_all(send_gate, "expert", split_axis=0, concat_axis=0, tiled=True),
    )
    x_blocks = lax.all_gather(arrived[0], "dp", axis=0, tiled=True)
    cot_blocks = lax.all_gather(arrived[1], "dp", axis=0, tiled=True)
    gate_blocks = lax.all_gather(arrived[2], "dp", axis=0, tiled=True)
    count = x_blocks.shape[0] * x_blocks.shape[1]
    x_rows = x_blocks.reshape(count, feat)
    cot_rows = cot_blocks.reshape(count, feat)
    gate_f = gate_blocks.reshape(count, 1).astype(jnp.float32)
    pre = jnp.dot(x_rows, w_first, preferred_element_type=jnp.float32)
    cdf, pdf = normal_parts(pre)
    hidden = (pre * cdf).astype(jnp.bfloat16)
    back = lax.dot_general(
        cot_rows, w_second, (((1,), (1,)), ((), ())), preferred_element_type=jnp.float32
    )
    scaled = (gate_f * cot_rows.astype(jnp.float32)).astype(jnp.bfloat16)
    grad_second = lax.dot_general(
        hidden, scaled, (((0,), (0,)), ((), ())), preferred_element_type=jnp.float32
    )
    pre_grad = (gate_f * back * (cdf + pre * pdf)).astype(jnp.bfloat16)
    grad_first = lax.dot_general(
        x_rows, pre_grad, (((0,), (0,)), ((), ())), preferred_element_type=jnp.float32
    )
    row_part = lax.dot_general(
        pre_grad, w_first, (((1,), (1,)), ((), ())), preferred_element_type=jnp.float32
    ).astype(jnp.bfloat16)
    gate_part = jnp.sum(hidden.astype(jnp.float32) * back, axis=1)
    row_sums = lax.psum_scatter(row_part, "dp", scatter_dimension=0, tiled=True)
    gate_sums = lax.psum_scatter(gate_part, "dp", scatter_dimension=0, tiled=True)
    row_back = row_sums.reshape(experts, cap, feat)
    gate_back = gate_sums.astype(jnp.bfloat16).reshape(experts, cap)
    back_rows, back_gate = (
        lax.all_to_all(row_back, "expert", split_axis=0, concat_axis=0, tiled=True),
        lax.all_to_all(gate_back, "expert", split_axis=0, concat_axis=0, tiled=True),
    )
    flat_back = back_rows.reshape(experts * cap, feat)
    per_assign = lax.dot_general(
        pick, flat_back, (((0,), (0,)), ((), ())), preferred_element_type=jnp.float32
    )
    token_grads = jnp.sum(per_assign.reshape(tok, 2, feat), axis=1).astype(jnp.bfloat16)
    gate_assign = lax.dot_general(
        pick,
        back_gate.reshape(experts * cap, 1),
        (((0,), (0,)), ((), ())),
        preferred_element_type=jnp.float32,
    )
    gate_grads = gate_assign.reshape(tok, 2).astype(jnp.bfloat16)
    grad_in_weights = grad_first.astype(jnp.bfloat16)[None]
    grad_out_weights = grad_second.astype(jnp.bfloat16)[None]
    return (token_grads, gate_grads, grad_in_weights, grad_out_weights)


def solution(mesh):
    in_specs = (
        P(("expert", "dp"), None),
        P(("expert", "dp"), None),
        P(("expert", "dp"), None),
        P(("expert", "dp"), None),
        P("expert", None, "dp"),
        P("expert", "dp", None),
    )
    out_specs = (
        P(("expert", "dp"), None),
        P(("expert", "dp"), None),
        P("expert", None, "dp"),
        P("expert", "dp", None),
    )
    return jax.shard_map(
        per_device, mesh=mesh, in_specs=in_specs, out_specs=out_specs, check_vma=False
    )
```

profile of v0, /device:TPU:0, one launch (start us, length us, event | category | flops | bytes accessed | tf_op | source)
XLA Modules:
  0.0 135.7 jit_solution(15528251252481260886)
XLA Ops:
  7.2 0.9 copy.25
  10.0 5.2 %all-to-all-start = ((bf16[8,1,8]{2,1,0:T(2,128)(2,1)}), bf16[8,1,8]{2,1,0:T(2,128)(2,1)S(1)}, u32[]{:S(2)}, u32[]{:S(2)}) async-start(bf16[8,1,8]{2,1,0:T(2,128)(2,1)} %all_to_all.31), calls=%async_computation | async-start | bytes 8192 | tf_op jit(solution)/shard_map/all_to_all | solution.py:50
  15.2 1.5 %broadcast_in_dim.18 = bf16[16,2,1664]{2,1,0:T(2,128)(2,1)} broadcast(bf16[16,1664]{1,0:T(8,128)(2,1)} %param.6), dimensions={0,2} | broadcast | bytes 159744 | tf_op jit(solution)/shard_map/broadcast_in_dim | solution.py:28
  16.7 0.9 reshape.124
  18.5 1.3 all-to-all-done
  19.8 4.0 %all-to-all-start.2 = ((bf16[8,8,1664]{2,1,0:T(8,128)(2,1)}), bf16[8,8,1664]{2,1,0:T(8,128)(2,1)}, u32[]{:S(2)}, u32[]{:S(2)}) async-start(bf16[8,8,1664]{2,1,0:T(8,128)(2,1)} %fusion.12), calls=%async_computation.2 | async-start | bytes 425984 | tf_op jit(solution)/shard_map/all_to_all | solution.py:48
  23.8 1.5 %broadcast_in_dim.8 = bf16[16,2,1664]{2,1,0:T(2,128)(2,1)} broadcast(bf16[16,1664]{1,0:T(8,128)(2,1)} %param.7), dimensions={0,2} | broadcast | bytes 159744 | tf_op jit(solution)/shard_map/broadcast_in_dim | solution.py:29
  25.3 0.9 reshape.121
  26.3 0.9 fusion.11
  27.1 12.1 %all-gather = bf16[32,1,8]{2,0,1:T(8,128)(2,1)S(1)} all-gather(bf16[8,1,8]{2,0,1:T(8,128)(2,1)S(1)} %copy.28), channel_id=2, replica_groups=mesh['expert'=8,'dp'=4] {'dp'}, dimensions={0}, use_global_device_ids=true | all-gather | bytes 640 | tf_op jit(solution)/shard_map/all_gather | solution.py:54
  39.3 4.1 %all-to-all-start.1 = ((bf16[8,8,1664]{2,1,0:T(8,128)(2,1)}), bf16[8,8,1664]{2,1,0:T(8,128)(2,1)}, u32[]{:S(2)}, u32[]{:S(2)}) async-start(bf16[8,8,1664]{2,1,0:T(8,128)(2,1)} %fusion.11), calls=%async_computation.1 | async-start | bytes 425984 | tf_op jit(solution)/shard_map/all_to_all | solution.py:49
  43.5 19.2 %all_gather.11 = bf16[32,8,1664]{2,1,0:T(8,128)(2,1)S(1)} all-gather(bf16[8,8,1664]{2,1,0:T(8,128)(2,1)} %all-to-all-done.2), channel_id=1, replica_groups=mesh['expert'=8,'dp'=4] {'dp'}, dimensions={0}, use_global_device_ids=true | all-gather | bytes 1064960 | tf_op jit(solution)/shard_map/all_gather | solution.py:52
  62.7 0.9 copy-done.1
  63.6 2.1 %fusion.2 = f32[256,1024]{1,0:T(8,128)} fusion(bf16[1,1664,1024]{2,1,0:T(8,128)(2,1)S(1)} %copy-done, bf16[32,8,1664]{2,1,0:T(8,128)(2,1)S(1)} %all_gather.11), kind=kOutput, calls=%fused_computation.4 | convolution fusion | flops 872415232 | bytes 5308416 | tf_op jit(solution)/shard_map/dot_general | solution.py:59
  65.8 19.5 %all_gather.10 = bf16[32,8,1664]{2,1,0:T(8,128)(2,1)S(1)} all-gather(bf16[8,8,1664]{2,1,0:T(8,128)(2,1)} %all-to-all-done.1), channel_id=1, replica_groups=mesh['expert'=8,'dp'=4] {'dp'}, dimensions={0}, use_global_device_ids=true | all-gather | bytes 1064960 | tf_op jit(solution)/shard_map/all_gather | solution.py:53
  85.3 4.8 %multiply_reduce_fusion = (f32[256]{0:T(256)S(1)}, bf16[256,1024]{1,0:T(8,128)(2,1)}, bf16[256,1024]{1,0:T(8,128)(2,1)S(1)}) fusion(f32[256,1024]{1,0:T(8,128)} %fusion.2, f32[256]{0:T(256)S(1)} %reshape.130, bf16[1,1024,1664]{2,1,0:T(8,128)(2,1)} %param.11, bf16[32,8,1664]{2,1,0:T(8,128)(2,1)S(1)} %all_gather.10), kind=kOutput, calls=%fused_computation.28 | convolution fusion | flops 876609280 | bytes 6359040 | tf_op jit(solution)/shard_map/dot_general | solution.py:62
  90.8 2.1 %fusion.8 = bf16[256,1664]{1,0:T(8,128)(2,1)} fusion(bf16[256,1024]{1,0:T(8,128)(2,1)S(1)} %get-tuple-element.6, bf16[1,1664,1024]{2,1,0:T(8,128)(2,1)S(1)} %copy-done), kind=kOutput, calls=%fused_computation.10 | convolution fusion | flops 872841216 | bytes 4784128 | tf_op jit(solution)/shard_map/dot_general | solution.py:73
  94.3 9.8 %all-reduce = bf16[256]{0:T(256)(128)(2,1)S(1)} all-reduce(f32[256]{0:T(256)S(1)} %get-tuple-element.4), channel_id=4, replica_groups=mesh['expert'=8,'dp'=4] {'dp'}, use_global_device_ids=true, to_apply=%region_4.0.clone | all-reduce | flops 256 | bytes 1536
  104.9 4.1 %all-to-all-start.4 = ((bf16[8,1,8]{2,1,0:T(2,128)(2,1)}), bf16[8,1,8]{2,1,0:T(2,128)(2,1)S(1)}, u32[]{:S(2)}, u32[]{:S(2)}) async-start(bf16[8,1,8]{2,1,0:T(2,128)(2,1)} %all_to_all.32), calls=%async_computation.5 | async-start | bytes 8192 | tf_op jit(solution)/shard_map/all_to_all | solution.py:83
  109.0 4.4 %fusion.7 = bf16[1,1024,1664]{2,1,0:T(8,128)(2,1)} fusion(bf16[256,1024]{1,0:T(8,128)(2,1)} %get-tuple-element.5, bf16[32,8,1664]{2,1,0:T(8,128)(2,1)} %copy-done.3, f32[256]{0:T(256)S(1)} %reshape.130), kind=kOutput, calls=%fused_computation.9 | convolution fusion | flops 875397120 | bytes 4785152 | tf_op jit(solution)/shard_map/dot_general | solution.py:66
  113.4 2.8 %fusion.6 = bf16[1,1664,1024]{2,1,0:T(8,128)(2,1)} fusion(bf16[256,1024]{1,0:T(8,128)(2,1)S(1)} %copy-done.6, bf16[32,8,1664]{2,1,0:T(8,128)(2,1)S(1)} %copy-done.2), kind=kOutput, calls=%fused_computation.8 | convolution fusion | flops 874119168 | bytes 4784128 | tf_op jit(solution)/shard_map/dot_general | solution.py:70
  116.6 4.0 %all-to-all-start.3 = ((bf16[8,8,1664]{2,1,0:T(8,128)(2,1)}), bf16[8,8,1664]{2,1,0:T(8,128)(2,1)}, u32[]{:S(2)}, u32[]{:S(2)}) async-start(bf16[8,8,1664]{2,1,0:T(8,128)(2,1)} %bitcast.57), calls=%async_computation.4 | async-start | bytes 425984 | tf_op jit(solution)/shard_map/all_to_all | solution.py:82
  121.4 5.7 %all-to-all-done.3 = bf16[8,8,1664]{2,1,0:T(8,128)(2,1)} async-done(((bf16[8,8,1664]{2,1,0:T(8,128)(2,1)}), bf16[8,8,1664]{2,1,0:T(8,128)(2,1)}, u32[]{:S(2)}, u32[]{:S(2)}) %all-to-all-start.3) | async-done | bytes 213024 | tf_op jit(solution)/shard_map/all_to_all | solution.py:82
  127.1 1.7 %convolution_reduce_fusion = bf16[16,1664]{1,0:T(8,128)(2,1)} fusion(bf16[8,8,1664]{2,1,0:T(8,128)(2,1)} %all-to-all-done.3, pred[16,2,64]{2,1,0:T(4,128)(4,1)S(1)} %eq.50), kind=kOutput, calls=%fused_computation.17 | convolution fusion | flops 6842368 | bytes 268288 | tf_op jit(solution)/shard_map/dot_general | solution.py:86
  (38 shorter events, 6.3 us)
Async XLA Ops:
  7.2 56.5 %copy-start = (bf16[1,1664,1024]{2,1,0:T(8,128)(2,1)S(1)}, bf16[1,1664,1024]{2,1,0:T(8,128)(2,1)}, u32[]{:S(2)}) copy-start(bf16[1,1664,1024]{2,1,0:T(8,128)(2,1)} %param.10) | copy-start | bytes 10223620
  10.0 9.8 %all-to-all-start = ((bf16[8,1,8]{2,1,0:T(2,128)(2,1)}), bf16[8,1,8]{2,1,0:T(2,128)(2,1)S(1)}, u32[]{:S(2)}, u32[]{:S(2)}) async-start(bf16[8,1,8]{2,1,0:T(2,128)(2,1)} %all_to_all.31), calls=%async_computation | async-start | bytes 8192 | tf_op jit(solution)/shard_map/all_to_all | solution.py:50
  19.8 19.6 %all-to-all-start.2 = ((bf16[8,8,1664]{2,1,0:T(8,128)(2,1)}), bf16[8,8,1664]{2,1,0:T(8,128)(2,1)}, u32[]{:S(2)}, u32[]{:S(2)}) async-start(bf16[8,8,1664]{2,1,0:T(8,128)(2,1)} %fusion.12), calls=%async_computation.2 | async-start | bytes 425984 | tf_op jit(solution)/shard_map/all_to_all | solution.py:48
  39.3 26.4 %all-to-all-start.1 = ((bf16[8,8,1664]{2,1,0:T(8,128)(2,1)}), bf16[8,8,1664]{2,1,0:T(8,128)(2,1)}, u32[]{:S(2)}, u32[]{:S(2)}) async-start(bf16[8,8,1664]{2,1,0:T(8,128)(2,1)} %fusion.11), calls=%async_computation.1 | async-start | bytes 425984 | tf_op jit(solution)/shard_map/all_to_all | solution.py:49
  43.4 73.2 %reduce-scatter.2.cloned.1.call-start = ((), (), s32[]{:S(2)}) async-start(), calls=%async_computation.6 | async-start | bytes 1064960 | tf_op jit(solution)/shard_map/reduce_scatter | solution.py:77
  62.7 0.9 copy-start.1
  85.3 4.8 %copy-start.3 = (bf16[32,8,1664]{2,1,0:T(8,128)(2,1)}, bf16[32,8,1664]{2,1,0:T(8,128)(2,1)S(1)}, u32[]{:S(2)}) copy-start(bf16[32,8,1664]{2,1,0:T(8,128)(2,1)S(1)} %all_gather.10) | copy-start | bytes 2555908
  90.0 0.8 copy-start.5
  90.0 3.0 %copy-start.4 = (u32[32]{0:T(128)S(1)}, u32[32]{0:T(128)}, u32[]{:S(2)}) copy-start(u32[32]{0:T(128)} %constant.23) | copy-start | bytes 388
  104.9 11.3 %all-to-all-start.4 = ((bf16[8,1,8]{2,1,0:T(2,128)(2,1)}), bf16[8,1,8]{2,1,0:T(2,128)(2,1)S(1)}, u32[]{:S(2)}, u32[]{:S(2)}) async-start(bf16[8,1,8]{2,1,0:T(2,128)(2,1)} %all_to_all.32), calls=%async_computation.5 | async-start | bytes 8192 | tf_op jit(solution)/shard_map/all_to_all | solution.py:83
  109.0 4.4 %copy-start.2 = (bf16[32,8,1664]{2,1,0:T(8,128)(2,1)S(1)}, bf16[32,8,1664]{2,1,0:T(8,128)(2,1)}, u32[]{:S(2)}) copy-start(bf16[32,8,1664]{2,1,0:T(8,128)(2,1)} %copy-done.1) | copy-start | bytes 2555908
  109.0 4.4 %copy-start.6 = (bf16[256,1024]{1,0:T(8,128)(2,1)S(1)}, bf16[256,1024]{1,0:T(8,128)(2,1)}, u32[]{:S(2)}) copy-start(bf16[256,1024]{1,0:T(8,128)(2,1)} %copy-done.5) | copy-start | bytes 1572868
  116.6 10.4 %all-to-all-start.3 = ((bf16[8,8,1664]{2,1,0:T(8,128)(2,1)}), bf16[8,8,1664]{2,1,0:T(8,128)(2,1)}, u32[]{:S(2)}, u32[]{:S(2)}) async-start(bf16[8,8,1664]{2,1,0:T(8,128)(2,1)} %bitcast.57), calls=%async_computation.4 | async-start | bytes 425984 | tf_op jit(solution)/shard_map/all_to_all | solution.py:82
Sparse Core Ops, SparseCore 0:
  93.1 23.5 reduce-scatter.1
where the time goes:
time: 136 us
  blocking collectives  60.6 us (45%)
  starting transfers between devices  21.4 us (16%)
  matrix products  20.1 us (15%)
  between operations  14.8 us (11%)
  local copies, waits for them, and re-layouts  10.7 us (8%)
  waiting for transfers between devices  7.34 us (5%)
    all_gather x1, blocking collectives, per_device(): cot_blocks = lax.all_gather(arrived[1], 'dp', axis=0, tiled=True)  19.5 us
    all_gather x1, blocking collectives, per_device(): x_blocks = lax.all_gather(arrived[0], 'dp', axis=0, tiled=True)  19.2 us
    all_gather x1, blocking collectives, per_device(): gate_blocks = lax.all_gather(arrived[2], 'dp', axis=0, tiled=True)  12.1 us
    unnamed x1, blocking collectives  9.82 us
    all_to_all x1, waiting for transfers between devices, per_device(): lax.all_to_all(row_back, 'expert', split_axis=0, concat_axis=0, tiled=True)  5.74 us
    all_to_all x1, starting transfers between devices, per_device(): lax.all_to_all(send_gate, 'expert', split_axis=0, concat_axis=0, tiled=True)  5.17 us
    dot_general x1, matrix products, per_device(): lax.dot_general(cot_rows, w_second, (((1,), (1,)), ((), ())), preferred_e...  4.77 us
    dot_general x1, matrix products, per_device(): lax.dot_general(hidden, scaled, (((0,), (0,)), ((), ())), preferred_eleme...  4.39 us
  transfers between devices with their start and end apart: 6, of which 3 were waited for; matrix products, arithmetic and copies ran while one was open for 13% of the time, Pallas kernels for 0%

commit v1 on v0

--- a/solution.py
+++ b/solution.py
@@ -1,7 +1,273 @@
+import functools
 import jax
 import jax.numpy as jnp
 from jax import lax
+from jax.experimental import pallas as pl
+from jax.experimental.pallas import tpu as pltpu
 from jax.sharding import PartitionSpec as P
+
+LANES = 128
+GATHER_BYTES = 8 << 20
+
+
+def flip(v, bit):
+    return v + bit - 2 * bit * ((v // bit) % 2)
+
+
+def fused_kernel(
+    tok, feat, hid, zs, cap,
+    pay_ref, w1_hbm, w2_hbm,
+    grads_ref, gate_ref, xr_ref, sc_ref, hid_ref, pg_ref,
+    G, W1, W2, CR, BE, TP, RC, S1, XA, SA, YA, YB, SB, XB, S3, ZR,
+    wsem, zs_s, zs_r, xs_s, xs_r, ys_s, ys_r, dxs, dxr, dys, dyr, cs_s, cs_r,
+    rc_s, rc_r, ra_s, ra_r, rb_s, rb_r, rz_s, rz_r,
+):
+    e = lax.axis_index("expert")
+    z = lax.axis_index("dp")
+    c, xb, yb = e % 2, (e // 2) % 2, (e // 4) % 2
+    ec, ex, ey, exy = flip(e, 1), flip(e, 2), flip(e, 4), flip(flip(e, 2), 4)
+    zp = [z]
+    for d in range(1, zs):
+        v = z
+        for b in range(8):
+            if (d >> b) & 1:
+                v = flip(v, 1 << b)
+        zp.append(v)
+    wide = 2 * feat + LANES
+    width = feat + LANES
+    hw = (wide // LANES // 2) * LANES
+    h0 = (width // LANES // 2) * LANES
+    blk = lambda ee, zz: ee * zs + zz
+
+    loads = [
+        pltpu.make_async_copy(w1_hbm, W1, wsem.at[0]),
+        pltpu.make_async_copy(w2_hbm, W2, wsem.at[1]),
+    ]
+    for l in loads:
+        l.start()
+    me = blk(e, z)
+    G[pl.ds(me, 1)] = pay_ref[...][None]
+
+    barrier = pltpu.get_barrier_semaphore()
+    peers = [(ec, z), (ex, z), (ey, z)] + [(e, zp[d]) for d in range(1, zs)]
+    for p in peers:
+        pl.semaphore_signal(barrier, inc=1, device_id=p, device_id_type=pl.DeviceIdType.MESH)
+    pl.semaphore_wait(barrier, len(peers))
+
+    def rcopy(src, dst, ss, rs, dev):
+        return pltpu.make_async_remote_copy(
+            src_ref=src, dst_ref=dst, send_sem=ss, recv_sem=rs,
+            device_id=dev, device_id_type=pl.DeviceIdType.MESH,
+        )
+
+    sends = []
+
+    def go(cp):
+        cp.start()
+        sends.append(cp)
+        return cp
+
+    zc = [None]
+    for d in range(1, zs):
+        zc.append(go(rcopy(G.at[me], G.at[me], zs_s.at[d], zs_r.at[d], (e, zp[d]))))
+    xc, yc, dx, dy, cc = [], [], [], [], []
+
+    def core_send(b, k):
+        cc.append(go(rcopy(G.at[b], G.at[b], cs_s.at[k], cs_r.at[k], (ec, z))))
+
+    def diag(j):
+        bx, by, bd = blk(ex, zp[j]), blk(ey, zp[j]), blk(exy, zp[j])
+        xc[j].wait_recv()
+        dy.append(go(rcopy(G.at[bx, :, pl.ds(0, hw)], G.at[bx, :, pl.ds(0, hw)],
+                           dys.at[j], dyr.at[j], (ey, z))))
+        core_send(bx, zs + j)
+        yc[j].wait_recv()
+        dx.append(go(rcopy(G.at[by, :, pl.ds(hw, wide - hw)], G.at[by, :, pl.ds(hw, wide - hw)],
+                           dxs.at[j], dxr.at[j], (ex, z))))
+        core_send(by, 2 * zs + j)
+
+    for j in range(zs):
+        b = blk(e, zp[j])
+        if j:
+            zc[j].wait_recv()
+        xc.append(go(rcopy(G.at[b], G.at[b], xs_s.at[j], xs_r.at[j], (ex, z))))
+        yc.append(go(rcopy(G.at[b], G.at[b], ys_s.at[j], ys_r.at[j], (ey, z))))
+        core_send(b, j)
+        if j:
+            diag(j - 1)
+    diag(zs - 1)
+    for j in range(zs):
+        dy[j].wait_recv()
+        dx[j].wait_recv()
+        core_send(blk(exy, zp[j]), 3 * zs + j)
+    for k in cc:
+        k.wait_recv()
+
+    blocks = G.shape[0]
+    per = blocks // 2
+    gt, gr = per * tok, per * cap
+    ef = e.astype(jnp.float32)
+    picks, metas = [], []
+    ti = lax.broadcasted_iota(jnp.int32, (gt, gt), 0)
+    tj = lax.broadcasted_iota(jnp.int32, (gt, gt), 1)
+    lower = jnp.where((ti // tok == tj // tok) & (tj < ti), 1.0, 0.0).astype(jnp.bfloat16)
+    base = ((lax.broadcasted_iota(jnp.int32, (gt, gr), 0) // tok) * cap).astype(jnp.float32)
+    lane = lax.broadcasted_iota(jnp.int32, (gt, gr), 1).astype(jnp.float32)
+    tdims = (((0,), (0,)), ((), ()))
+    for g in range(2):
+        m = G[g * per:(g + 1) * per, :, 2 * feat:].reshape(gt, LANES).astype(jnp.float32)
+        m0 = m[:, 0:1] == ef
+        m1 = m[:, 1:2] == ef
+        mask = jnp.where(m0 | m1, 1.0, 0.0)
+        gtok = jnp.where(m0, m[:, 2:3], 0.0) + jnp.where(m1, m[:, 3:4], 0.0)
+        slot = jnp.dot(lower, jnp.broadcast_to(mask, (gt, gr)).astype(jnp.bfloat16),
+                       preferred_element_type=jnp.float32)
+        pick = jnp.where((slot + base == lane) & (mask > 0.0), 1.0, 0.0).astype(jnp.bfloat16)
+        picks.append(pick)
+        metas.append(m)
+        gate = lax.dot_general(pick, jnp.broadcast_to(gtok, (gt, LANES)).astype(jnp.bfloat16),
+                               tdims, preferred_element_type=jnp.float32)
+        BE[g * gr:(g + 1) * gr, :] = gate
+        xg = G[g * per:(g + 1) * per, :, 0:feat].reshape(gt, feat)
+        xr_ref[g * gr:(g + 1) * gr, :] = lax.dot_general(
+            pick, xg, tdims, preferred_element_type=jnp.float32).astype(jnp.bfloat16)
+        cg = G[g * per:(g + 1) * per, :, feat:2 * feat].reshape(gt, feat)
+        cr = lax.dot_general(pick, cg, tdims, preferred_element_type=jnp.float32)
+        CR[g * gr:(g + 1) * gr, :] = cr.astype(jnp.bfloat16)
+        sc_ref[g * gr:(g + 1) * gr, :] = (gate[:, 0:1] * cr).astype(jnp.bfloat16)
+
+    for l in loads:
+        l.wait()
+    rows = 2 * gr
+    step = min(hid, 256)
+
+    def hidden_step(i, acc):
+        f = pl.multiple_of(i * step, step)
+        pre = jnp.dot(xr_ref[...], W1[:, pl.ds(f, step)], preferred_element_type=jnp.float32)
+        back = lax.dot_general(CR[...], W2[pl.ds(f, step), :], (((1,), (1,)), ((), ())),
+                               preferred_element_type=jnp.float32)
+        cdf = 0.5 * (1.0 + lax.erf(pre * 0.7071067811865476))
+        pdf = 0.3989422804014327 * jnp.exp(-0.5 * pre * pre)
+        h = (pre * cdf).astype(jnp.bfloat16)
+        hid_ref[:, pl.ds(f, step)] = h
+        pg_ref[:, pl.ds(f, step)] = (BE[:, 0:1] * back * (cdf + pre * pdf)).astype(jnp.bfloat16)
+        return acc + jnp.sum(h.astype(jnp.float32) * back, axis=1, keepdims=True)
+
+    gsum = lax.fori_loop(0, hid // step, hidden_step, jnp.zeros((rows, 1), jnp.float32))
+    hi = gsum.astype(jnp.bfloat16).astype(jnp.float32)
+    li = lax.broadcasted_iota(jnp.int32, (rows, LANES), 1)
+    extra = jnp.where(li < 2, hi, gsum - hi).astype(jnp.bfloat16)
+
+    def place(lo, hi_):
+        n = min(hi_, feat) - lo
+        part = lax.dot_general(pg_ref[...], W1[lo:lo + n, :], (((1,), (1,)), ((), ())),
+                               preferred_element_type=jnp.float32).astype(jnp.bfloat16)
+        for g in range(2):
+            t = jnp.dot(picks[g], part[g * gr:(g + 1) * gr], preferred_element_type=jnp.float32)
+            TP[2 * g:2 * g + 2, :, :, :, lo:lo + n] = t.astype(jnp.bfloat16).reshape(2, 2, zs, tok, n)
+            if hi_ > feat:
+                v = jnp.dot(picks[g], extra[g * gr:(g + 1) * gr], preferred_element_type=jnp.float32)
+                tl = lax.broadcasted_iota(jnp.int32, (gt, LANES), 1)
+                m = metas[g]
+                own = jnp.where(tl % 2 == 0, m[:, 0:1], m[:, 1:2]) == ef
+                v = jnp.where(own & (tl < 4), v, 0.0)
+                TP[2 * g:2 * g + 2, :, :, :, feat:] = v.astype(jnp.bfloat16).reshape(2, 2, zs, tok, LANES)
+
+    def core_swap(i, lo, n):
+        return go(rcopy(TP.at[:, 1 - c, :, :, pl.ds(lo, n)], RC.at[:, :, :, pl.ds(lo, n)],
+                        rc_s.at[i], rc_r.at[i], (ec, z)))
+
+    def core_add(lo, n):
+        s = (TP[:, pl.ds(c, 1), :, :, lo:lo + n].reshape(4, zs, tok, n).astype(jnp.float32)
+             + RC[:, :, :, lo:lo + n].astype(jnp.float32))
+        S1[:, :, :, :, lo:lo + n] = s.astype(jnp.bfloat16).reshape(2, 2, zs, tok, n)
+
+    n1 = width - h0
+    f32 = jnp.float32
+    place(0, h0)
+    s0 = core_swap(0, 0, h0)
+    place(h0, width)
+    s1 = core_swap(1, h0, n1)
+    s0.wait_recv()
+    core_add(0, h0)
+    a0 = go(rcopy(S1.at[:, 1 - xb, :, :, pl.ds(0, h0)], XA, ra_s.at[0], ra_r.at[0], (ex, z)))
+    s1.wait_recv()
+    core_add(h0, n1)
+    a1 = go(rcopy(S1.at[1 - yb, :, :, :, pl.ds(h0, n1)], YB, ra_s.at[1], ra_r.at[1], (ey, z)))
+    a0.wait_recv()
+    SA[...] = (S1[:, pl.ds(xb, 1), :, :, 0:h0].reshape(2, zs, tok, h0).astype(f32)
+               + XA[...].astype(f32)).astype(jnp.bfloat16)
+    b0 = go(rcopy(SA.at[1 - yb], YA, rb_s.at[0], rb_r.at[0], (ey, z)))
+    a1.wait_recv()
+    SB[...] = (S1[pl.ds(yb, 1), :, :, :, h0:].reshape(2, zs, tok, n1).astype(f32)
+               + YB[...].astype(f32)).astype(jnp.bfloat16)
+    b1 = go(rcopy(SB.at[1 - xb], XB, rb_s.at[1], rb_r.at[1], (ex, z)))
+    b0.wait_recv()
+    S3[:, :, 0:h0] = (SA[pl.ds(yb, 1)].reshape(zs, tok, h0).astype(f32)
+                      + YA[...].astype(f32)).astype(jnp.bfloat16)
+    b1.wait_recv()
+    S3[:, :, h0:] = (SB[pl.ds(xb, 1)].reshape(zs, tok, n1).astype(f32)
+                     + XB[...].astype(f32)).astype(jnp.bfloat16)
+    zcs = [go(rcopy(S3.at[zp[d]], ZR.at[d - 1], rz_s.at[d], rz_r.at[d], (e, zp[d])))
+           for d in range(1, zs)]
+    total = S3[pl.ds(z, 1)].reshape(tok, width).astype(f32)
+    for d in range(1, zs):
+        zcs[d - 1].wait_recv()
+        total = total + ZR[d - 1].astype(f32)
+    grads_ref[...] = total[:, 0:feat].astype(jnp.bfloat16)
+    gate_ref[...] = total[:, feat:]
+    for s in sends:
+        s.wait_send()
+
+
+def fused(tokens, cotangent, expert_ids, gates, w_in, w_out):
+    tok, feat = tokens.shape
+    experts, zs = lax.axis_size("expert"), lax.axis_size("dp")
+    hid = w_in.shape[2]
+    cap = max(2, 4 * tok // experts)
+    bf = jnp.bfloat16
+    meta = jnp.concatenate(
+        [expert_ids.astype(bf), gates, jnp.zeros((tok, LANES - 4), bf)], axis=1)
+    pay = jnp.concatenate([tokens, cotangent, meta], axis=1)
+    blocks = experts * zs
+    rows = blocks * cap
+    width = feat + LANES
+    h0 = (width // LANES // 2) * LANES
+    n1 = width - h0
+    vm = pl.BlockSpec(memory_space=pltpu.VMEM)
+    hbm = pl.BlockSpec(memory_space=pl.ANY)
+    dma = lambda n: pltpu.SemaphoreType.DMA((n,))
+    V = lambda *s: pltpu.VMEM(s, bf)
+    sd = jax.ShapeDtypeStruct
+    grads, gate, xr, sc, hd, pg = pl.pallas_call(
+        functools.partial(fused_kernel, tok, feat, hid, zs, cap),
+        out_shape=(
+            sd((tok, feat), bf), sd((tok, LANES), jnp.float32), sd((rows, feat), bf),
+            sd((rows, feat), bf), sd((rows, hid), bf), sd((rows, hid), bf),
+        ),
+        in_specs=[vm, hbm, hbm],
+        out_specs=(vm,) * 6,
+        scratch_shapes=[
+            V(blocks, tok, 2 * feat + LANES), V(feat, hid), V(hid, feat), V(rows, feat),
+            pltpu.VMEM((rows, LANES), jnp.float32),
+            V(4, 2, zs, tok, width), V(4, zs, tok, width), V(2, 2, zs, tok, width),
+            V(2, zs, tok, h0), V(2, zs, tok, h0), V(zs, tok, h0),
+            V(2, zs, tok, n1), V(2, zs, tok, n1), V(zs, tok, n1),
+            V(zs, tok, width), V(zs - 1, tok, width),
+            dma(2), dma(zs), dma(zs), dma(zs), dma(zs), dma(zs), dma(zs),
+            dma(zs), dma(zs), dma(zs), dma(zs), dma(4 * zs), dma(4 * zs),
+            dma(2), dma(2), dma(2), dma(2), dma(2), dma(2), dma(zs), dma(zs),
+        ],
+        compiler_params=pltpu.CompilerParams(
+            collective_id=0, has_side_effects=True, vmem_limit_bytes=48 << 20),
+        cost_estimate=pl.CostEstimate(
+            flops=6 * rows * feat * hid, bytes_accessed=4 * feat * hid, transcendentals=0),
+    )(pay, w_in[0], w_out[0])
+    dims = (((0,), (0,)), ((), ()))
+    g1 = lax.dot_general(xr, pg, dims, preferred_element_type=jnp.float32).astype(bf)
+    g2 = lax.dot_general(hd, sc, dims, preferred_element_type=jnp.float32).astype(bf)
+    gate_grads = (gate[:, 0:2] + gate[:, 2:4]).astype(bf)
+    return grads, gate_grads, g1[None], g2[None]
 
 
 def normal_parts(pre):
@@ -114,6 +380,19 @@
         P("expert", None, "dp"),
         P("expert", "dp", None),
     )
-    return jax.shard_map(
-        per_device, mesh=mesh, in_specs=in_specs, out_specs=out_specs, check_vma=False
-    )
+    sizes = dict(mesh.shape)
+
+    def run(tokens, *rest):
+        zs = sizes["dp"]
+        row_bytes = 2 * (2 * tokens.shape[1] + LANES)
+        small = tokens.shape[0] * row_bytes <= GATHER_BYTES
+        cube = sizes["expert"] == 8 and zs > 1 and zs & (zs - 1) == 0
+        plan = fused if small and cube else per_device
+        return mapped(plan)(tokens, *rest)
+
+    def mapped(plan):
+        return jax.shard_map(
+            plan, mesh=mesh, in_specs=in_specs, out_specs=out_specs, check_vma=False
+        )
+
+    return run

time: 136 us -> 61.4 us (0.45)
  blocking collectives: 60.6 us -> 0 us
  Pallas kernels: 0 us -> 51.1 us
  starting transfers between devices: 21.4 us -> 0 us
  matrix products: 20.1 us -> 5.74 us
  between operations: 14.8 us -> 0.64 us
  local copies, waits for them, and re-layouts: 10.7 us -> 3 us
  waiting for transfers between devices: 7.34 us -> 0 us
    pallas_call x0 -> x1, Pallas kernels: none -> 51.1 us  [fused(): pl.pallas_call(functools.partial(fused_kernel, tok, feat, hid, zs, cap),...]
    all_gather x3 -> x0, blocking collectives: 50.8 us -> none  [the longest x1 19.5 us: per_device(): cot_blocks = lax.all_gather(arrived[1], 'dp', axis=0, tiled=True)]
    all_to_all x5 -> x0, starting transfers between devices: 21.4 us -> none  [the longest x1 5.17 us: per_device(): lax.all_to_all(send_gate, 'expert', split_axis=0, concat_axis=0, tiled=True)]
    dot_general x11 -> x2, matrix products: 20.1 us -> 5.74 us  [the longest x1 2.92 us: fused(): lax.dot_general(hd, sc, dims, preferred_element_type=jnp.float32).astype(bf)]
    unnamed x1 -> x0, blocking collectives: 9.82 us -> none
    all_to_all x5 -> x0, waiting for transfers between devices: 7.01 us -> none  [the longest x1 5.74 us: per_device(): lax.all_to_all(row_back, 'expert', split_axis=0, concat_axis=0, tiled=True)]
    broadcast_in_dim x2 -> x1, local copies, waits for them, and re-layouts: 3.02 us -> 0.01 us  [fused(): jnp.zeros((tok, LANES - 4), bf)]
    unnamed x18 -> x3, local copies, waits for them, and re-layouts: 4.04 us -> 1.97 us
  transfers between devices with their start and end apart: 6 -> 0, of which waited for: 3 -> 0; matrix products, arithmetic and copies ran while one was open for 13% -> 0% of each run, Pallas kernels for 0% -> 0%
where the time goes in v1:
time: 61.4 us; the launch traced here: 61.2 us
  Pallas kernels  51.1 us (83%)
  matrix products  5.74 us (9%)
  local copies, waits for them, and re-layouts  3 us (5%)
  other arithmetic  0.76 us (1%)
  between operations  0.64 us (1%)
    pallas_call x1, Pallas kernels, fused(): pl.pallas_call(functools.partial(fused_kernel, tok, feat, hid, zs, cap),...  51.1 us
    dot_general x1, matrix products, fused(): lax.dot_general(hd, sc, dims, preferred_element_type=jnp.float32).astype(bf)  2.92 us
    dot_general x1, matrix products, fused(): lax.dot_general(xr, pg, dims, preferred_element_type=jnp.float32).astype(bf)  2.82 us
    unnamed x3, local copies, waits for them, and re-layouts  1.97 us

profile of v1, /device:TPU:0, one launch (start us, length us, event | category | flops | bytes accessed | tf_op | source)
XLA Modules:
  0.0 61.2 jit_solution(14953362391348512718)
XLA Ops:
  0.6 0.7 %convert_element_type.12 = bf16[16,2]{0,1:T(2,128)(2,1)S(1)} convert(s32[16,2]{0,1:T(2,128)} %param.8) | non-fusion elementwise | flops 32 | bytes 192 | tf_op jit(solution)/shard_map/convert_element_type | solution.py:230
  1.3 0.1 copy.10
  1.4 0.7 %copy.11 = bf16[16,2]{1,0:T(8,128)(2,1)S(1)} copy(bf16[16,2]{0,1:T(2,128)(2,1)} %param.9) | data formatting | bytes 128 | tf_op args[3]
  2.2 0.9 %concatenate.3.pay_ref = bf16[16,3456]{1,0:T(8,128)(2,1)S(1)} concatenate(bf16[16,1664]{1,0:T(8,128)(2,1)} %param.6, bf16[16,1664]{1,0:T(8,128)(2,1)} %param.7, bf16[16,2]{1,0:T(8,128)(2,1)S(1)} %copy.10, bf16[16,2]{1,0:T(8,128)(2,1)S(1)} %copy.11, bf16[16,124]{1,0:T(8,128)(2,1)S(1)} %broadcast_in_dim.9), dimensions={1} | concatenate | bytes 221184 | tf_op jit(solution)/shard_map/concatenate | solution.py:231
  3.1 51.1 %shard_map.93 = (bf16[16,1664]{1,0:T(8,128)(2,1)S(1)}, f32[16,128]{1,0:T(8,128)S(1)}, bf16[256,1664]{1,0:T(8,128)(2,1)S(1)}, bf16[256,1664]{1,0:T(8,128)(2,1)S(1...) custom-call(bf16[16,3456]{1,0:T(8,128)(2,1)S(1)} %concatenate.3.pay_ref, bf16[1664,1024]{1,0:T(8,128)(2,1)} %bitcast.10, ...), custom_call_target="tpu_custom_call" | custom-call | flops 2617245696 | bytes 6815744 | tf_op jit(solution)/shard_map/pallas_call | solution.py:242
  54.2 0.1 add_convert_fusion
  54.2 0.6 copy.12
  54.8 2.8 %fusion = bf16[1,1664,1024]{2,1,0:T(8,128)(2,1)} fusion(bf16[256,1664]{1,0:T(8,128)(2,1)S(1)} %get-tuple-element.12, bf16[256,1024]{1,0:T(8,128)(2,1)S(1)} %get-tuple-element.13), kind=kOutput, calls=%fused_computation.2 | convolution fusion | flops 874119168 | bytes 4784128 | tf_op jit(solution)/shard_map/dot_general | solution.py:267
  57.7 2.9 %fusion.1 = bf16[1,1024,1664]{2,1,0:T(8,128)(2,1)} fusion(bf16[256,1024]{1,0:T(8,128)(2,1)S(1)} %get-tuple-element.14, bf16[256,1664]{1,0:T(8,128)(2,1)S(1)} %get-tuple-element.15), kind=kOutput, calls=%fused_computation.3 | convolution fusion | flops 874119168 | bytes 4784128 | tf_op jit(solution)/shard_map/dot_general | solution.py:268
  60.6 0.6 %copy.14 = bf16[16,1664]{1,0:T(8,128)(2,1)} copy(bf16[16,1664]{1,0:T(8,128)(2,1)S(1)} %get-tuple-element.24) | data formatting | bytes 106496
  (1 shorter events, 0.0 us)

commit v2 on v0

--- a/solution.py
+++ b/solution.py
@@ -1,7 +1,317 @@
+import functools
 import jax
 import jax.numpy as jnp
 from jax import lax
+from jax.experimental import pallas as pl
+from jax.experimental.pallas import tpu as pltpu
 from jax.sharding import PartitionSpec as P
+
+LANES = 128
+GATHER_BYTES = 8 << 20
+
+
+def flip(v, bit):
+    return v + bit - 2 * bit * ((v // bit) % 2)
+
+
+def fused_kernel(
+    tok, feat, hid, zs, cap, chunks,
+    tok_ref, cot_ref, ids_ref, gates_ref, w1_hbm, w2_hbm,
+    grads_ref, gate_ref, xr_ref, sc_ref, hid_ref, pg_ref,
+    G, W1, W2, CR, BE, TP, RC, S1, A1, A2, A3, S3, ZR,
+    wsem, zs_s, zs_r, xs_s, xs_r, ys_s, ys_r, dxs, dxr, dys, dyr, cs_s, cs_r,
+    rc_s, rc_r, ra_s, ra_r, rb_s, rb_r, rz_s, rz_r,
+):
+    f32, bf = jnp.float32, jnp.bfloat16
+    e = lax.axis_index("expert")
+    z = lax.axis_index("dp")
+    experts = G.shape[0] // zs
+    c, xb, yb = e % 2, (e // 2) % 2, (e // 4) % 2
+    ec, ex, ey, exy = flip(e, 1), flip(e, 2), flip(e, 4), flip(flip(e, 2), 4)
+    zp = [z]
+    for d in range(1, zs):
+        v = z
+        for b in range(8):
+            if (d >> b) & 1:
+                v = flip(v, 1 << b)
+        zp.append(v)
+    wide = 2 * feat + LANES
+    hw = (wide // LANES // 2) * LANES
+    blk = lambda ee, j: j * experts + ee
+
+    loads = [
+        pltpu.make_async_copy(w1_hbm, W1, wsem.at[0]),
+        pltpu.make_async_copy(w2_hbm, W2, wsem.at[1]),
+    ]
+    for l in loads:
+        l.start()
+    eye = lax.broadcasted_iota(jnp.int32, (tok, tok), 0) == lax.broadcasted_iota(
+        jnp.int32, (tok, tok), 1)
+    col = lambda r: jnp.sum(jnp.where(eye, r, 0.0), axis=1, keepdims=True)
+    ids_f, gates_f = ids_ref[...].astype(f32), gates_ref[...].astype(f32)
+    ln = lax.broadcasted_iota(jnp.int32, (tok, LANES), 1)
+    meta = jnp.zeros((tok, LANES), f32)
+    for k, r in enumerate((ids_f[0:1], ids_f[1:2], gates_f[0:1], gates_f[1:2])):
+        meta = jnp.where(ln == k, col(r), meta)
+    G[pl.ds(e, 1), :, 0:feat] = tok_ref[...][None]
+    G[pl.ds(e, 1), :, feat:2 * feat] = cot_ref[...][None]
+    G[pl.ds(e, 1), :, 2 * feat:] = meta.astype(bf)[None]
+
+    barrier = pltpu.get_barrier_semaphore()
+    peers = [(ec, z), (ex, z), (ey, z)] + [(e, zp[d]) for d in range(1, zs)]
+    for p in peers:
+        pl.semaphore_signal(barrier, inc=1, device_id=p, device_id_type=pl.DeviceIdType.MESH)
+    pl.semaphore_wait(barrier, len(peers))
+
+    sends = []
+
+    def go(src, dst, ss, rs, dev):
+        cp = pltpu.make_async_remote_copy(
+            src_ref=src, dst_ref=dst, send_sem=ss, recv_sem=rs,
+            device_id=dev, device_id_type=pl.DeviceIdType.MESH,
+        )
+        cp.start()
+        sends.append(cp)
+        return cp
+
+    xc, yc, dx, dy, cc = [], [], [], [], {}
+    zc = [None]
+
+    def core_send(b, j, k):
+        cc[j, k] = go(G.at[b], G.at[b], cs_s.at[k * zs + j], cs_r.at[k * zs + j], (ec, z))
+
+    def plane(j):
+        b = blk(e, j)
+        xc.append(go(G.at[b], G.at[b], xs_s.at[j], xs_r.at[j], (ex, z)))
+        yc.append(go(G.at[b], G.at[b], ys_s.at[j], ys_r.at[j], (ey, z)))
+        core_send(b, j, 0)
+
+    def diag(j):
+        bx, by = blk(ex, j), blk(ey, j)
+        xc[j].wait_recv()
+        v = G.at[bx, :, pl.ds(0, hw)]
+        dy.append(go(v, v, dys.at[j], dyr.at[j], (ey, z)))
+        core_send(bx, j, 1)
+        yc[j].wait_recv()
+        v = G.at[by, :, pl.ds(hw, wide - hw)]
+        dx.append(go(v, v, dxs.at[j], dxr.at[j], (ex, z)))
+        core_send(by, j, 2)
+
+    def finish(j):
+        dy[j].wait_recv()
+        dx[j].wait_recv()
+        core_send(blk(exy, j), j, 3)
+
+    per = G.shape[0] // 2
+    zh = zs // 2
+    gt, gr = per * tok, per * cap
+    ef = e.astype(f32)
+    ti = lax.broadcasted_iota(jnp.int32, (gt, gt), 0)
+    tj = lax.broadcasted_iota(jnp.int32, (gt, gt), 1)
+    lower = jnp.where((ti // tok == tj // tok) & (tj < ti), 1.0, 0.0).astype(bf)
+    base = ((lax.broadcasted_iota(jnp.int32, (gt, gr), 0) // tok) * cap).astype(f32)
+    lane = lax.broadcasted_iota(jnp.int32, (gt, gr), 1).astype(f32)
+    tdims = (((0,), (0,)), ((), ()))
+    ndims = (((1,), (1,)), ((), ()))
+    picks, metas, gsums = [], [], [None, None]
+    step = min(hid, 256)
+
+    def pick_group(g):
+        for j in range(g * zh, (g + 1) * zh):
+            for k in range(4):
+                cc[j, k].wait_recv()
+        m = G[g * per:(g + 1) * per, :, 2 * feat:].reshape(gt, LANES).astype(f32)
+        m0 = m[:, 0:1] == ef
+        m1 = m[:, 1:2] == ef
+        mask = jnp.where(m0 | m1, 1.0, 0.0)
+        gtok = jnp.where(m0, m[:, 2:3], 0.0) + jnp.where(m1, m[:, 3:4], 0.0)
+        slot = jnp.dot(lower, jnp.broadcast_to(mask, (gt, gr)).astype(bf),
+                       preferred_element_type=f32)
+        pick = jnp.where((slot + base == lane) & (mask > 0.0), 1.0, 0.0).astype(bf)
+        picks.append(pick)
+        metas.append(m)
+        gate = lax.dot_general(pick, jnp.broadcast_to(gtok, (gt, LANES)).astype(bf),
+                               tdims, preferred_element_type=f32)
+        sl = slice(g * gr, (g + 1) * gr)
+        BE[sl, :] = gate
+        xg = G[g * per:(g + 1) * per, :, 0:feat].reshape(gt, feat)
+        xr_ref[sl, :] = lax.dot_general(pick, xg, tdims, preferred_element_type=f32).astype(bf)
+        cg = G[g * per:(g + 1) * per, :, feat:2 * feat].reshape(gt, feat)
+        cr = lax.dot_general(pick, cg, tdims, preferred_element_type=f32)
+        CR[sl, :] = cr.astype(bf)
+        sc_ref[sl, :] = (gate[:, 0:1] * cr).astype(bf)
+
+    def hidden_step(g, i):
+        sl, fs = slice(g * gr, (g + 1) * gr), slice(i * step, (i + 1) * step)
+        pre = jnp.dot(xr_ref[sl, :], W1[:, fs], preferred_element_type=f32)
+        back = lax.dot_general(CR[sl, :], W2[fs, :], ndims, preferred_element_type=f32)
+        cdf = 0.5 * (1.0 + lax.erf(pre * 0.7071067811865476))
+        pdf = 0.3989422804014327 * jnp.exp(-0.5 * pre * pre)
+        h = (pre * cdf).astype(bf)
+        hid_ref[sl, fs] = h
+        pg_ref[sl, fs] = (BE[sl, 0:1] * back * (cdf + pre * pdf)).astype(bf)
+        t = jnp.sum(h.astype(f32) * back, axis=1, keepdims=True)
+        gsums[g] = t if gsums[g] is None else gsums[g] + t
+
+    for d in range(1, zs):
+        zc.append(go(G.at[blk(e, 0)], G.at[blk(e, d)], zs_s.at[d], zs_r.at[d], (e, zp[d])))
+    for j in range(zs):
+        if j:
+            zc[j].wait_recv()
+        plane(j)
+        if j:
+            diag(j - 1)
+    for j in range(zh):
+        finish(j)
+    steps = hid // step
+    pick_group(0)
+    for l in loads:
+        l.wait()
+    for i in range(steps // 2):
+        hidden_step(0, i)
+    diag(zs - 1)
+    for j in range(zh, zs - 1):
+        finish(j)
+    for i in range(steps // 2, steps):
+        hidden_step(0, i)
+    finish(zs - 1)
+    pick_group(1)
+    for i in range(steps):
+        hidden_step(1, i)
+
+    def place(i):
+        lo, w = chunks[i]
+        n = min(lo + w, feat) - lo
+        part = lax.dot_general(pg_ref[...], W1[lo:lo + n, :], ndims,
+                               preferred_element_type=f32).astype(bf)
+        for g in range(2):
+            js, rs = slice(g * zh, (g + 1) * zh), slice(g * gr, (g + 1) * gr)
+            t = jnp.dot(picks[g], part[rs], preferred_element_type=f32)
+            TP[js, :, :, :, :, lo:lo + n] = t.astype(bf).reshape(zh, 2, 2, 2, tok, n)
+            if lo + w > feat:
+                hi = gsums[g].astype(bf).astype(f32)
+                li = lax.broadcasted_iota(jnp.int32, (gr, LANES), 1)
+                extra = jnp.where(li < 2, hi, gsums[g] - hi).astype(bf)
+                v = jnp.dot(picks[g], extra, preferred_element_type=f32)
+                tl = lax.broadcasted_iota(jnp.int32, (gt, LANES), 1)
+                m = metas[g]
+                own = jnp.where(tl % 2 == 0, m[:, 0:1], m[:, 1:2]) == ef
+                v = jnp.where(own & (tl < 4), v, 0.0)
+                TP[js, :, :, :, :, feat:] = v.astype(bf).reshape(zh, 2, 2, 2, tok, LANES)
+        ds = pl.ds(lo, w)
+        swaps.append(go(TP.at[:, :, :, 1 - c, :, ds], RC.at[:, :, :, :, ds],
+                        rc_s.at[i], rc_r.at[i], (ec, z)))
+
+    swaps, firsts, seconds, lasts = [], [], [], []
+
+    def after_core(i):
+        lo, w = chunks[i]
+        ds = pl.ds(lo, w)
+        swaps[i].wait_recv()
+        s = (TP[:, :, :, pl.ds(c, 1), :, lo:lo + w].reshape(zs, 2, 2, tok, w).astype(f32)
+             + RC[:, :, :, :, lo:lo + w].astype(f32))
+        S1[:, :, :, :, lo:lo + w] = s.astype(bf)
+        if i % 2 == 0:
+            src, dev = S1.at[:, :, 1 - xb, :, ds], (ex, z)
+        else:
+            src, dev = S1.at[:, 1 - yb, :, :, ds], (ey, z)
+        firsts.append(go(src, A1.at[:, :, :, ds], ra_s.at[i], ra_r.at[i], dev))
+
+    def after_first(i):
+        lo, w = chunks[i]
+        ds = pl.ds(lo, w)
+        firsts[i].wait_recv()
+        if i % 2 == 0:
+            mine, other, dev = S1[:, :, pl.ds(xb, 1), :, lo:lo + w], 1 - yb, (ey, z)
+        else:
+            mine, other, dev = S1[:, pl.ds(yb, 1), :, :, lo:lo + w], 1 - xb, (ex, z)
+        A2[:, :, :, lo:lo + w] = (mine.reshape(zs, 2, tok, w).astype(f32)
+                                  + A1[:, :, :, lo:lo + w].astype(f32)).astype(bf)
+        seconds.append(go(A2.at[:, other, :, ds], A3.at[:, :, ds],
+                          rb_s.at[i], rb_r.at[i], dev))
+
+    def after_second(i):
+        lo, w = chunks[i]
+        ds = pl.ds(lo, w)
+        seconds[i].wait_recv()
+        own = yb if i % 2 == 0 else xb
+        S3[:, :, lo:lo + w] = (A2[:, pl.ds(own, 1), :, lo:lo + w].reshape(zs, tok, w).astype(f32)
+                               + A3[:, :, lo:lo + w].astype(f32)).astype(bf)
+        lasts.append([go(S3.at[d, :, ds], ZR.at[d - 1, :, ds],
+                         rz_s.at[i * zs + d], rz_r.at[i * zs + d], (e, zp[d]))
+                      for d in range(1, zs)])
+
+    n = len(chunks)
+    for t in range(n + 5):
+        for lag, stage in ((0, place), (1, after_core), (3, after_first), (5, after_second)):
+            if 0 <= t - lag < n:
+                stage(t - lag)
+    for i, (lo, w) in enumerate(chunks):
+        total = S3[0, :, lo:lo + w].astype(f32)
+        for d in range(1, zs):
+            lasts[i][d - 1].wait_recv()
+            total = total + ZR[d - 1, :, lo:lo + w].astype(f32)
+        m = min(lo + w, feat) - lo
+        grads_ref[:, lo:lo + m] = total[:, 0:m].astype(bf)
+        if m < w:
+            row = lambda k: jnp.sum(
+                jnp.where(eye, total[:, m + k:m + k + 1] + total[:, m + k + 2:m + k + 3], 0.0),
+                axis=0, keepdims=True)
+            first = lax.broadcasted_iota(jnp.int32, (2, tok), 0) == 0
+            gate_ref[...] = jnp.where(first, row(0), row(1)).astype(bf)
+    for s in sends:
+        s.wait_send()
+
+
+def fused(tokens, cotangent, expert_ids, gates, w_in, w_out):
+    tok, feat = tokens.shape
+    experts, zs = lax.axis_size("expert"), lax.axis_size("dp")
+    hid = w_in.shape[2]
+    cap = max(2, 4 * tok // experts)
+    bf = jnp.bfloat16
+    blocks = experts * zs
+    rows = blocks * cap
+    width = feat + LANES
+    tiles = width // LANES
+    a, b = tiles // 4, tiles // 2 - tiles // 4
+    widths = (a, b, b, tiles - a - 2 * b)
+    chunks, at = [], 0
+    for w in widths:
+        chunks.append((at * LANES, w * LANES))
+        at += w
+    nc = len(chunks)
+    vm = pl.BlockSpec(memory_space=pltpu.VMEM)
+    hbm = pl.BlockSpec(memory_space=pl.ANY)
+    dma = lambda n: pltpu.SemaphoreType.DMA((n,))
+    V = lambda *s: pltpu.VMEM(s, bf)
+    sd = jax.ShapeDtypeStruct
+    grads, gate, xr, sc, hd, pg = pl.pallas_call(
+        functools.partial(fused_kernel, tok, feat, hid, zs, cap, tuple(chunks)),
+        out_shape=(
+            sd((tok, feat), bf), sd((2, tok), bf), sd((rows, feat), bf),
+            sd((rows, feat), bf), sd((rows, hid), bf), sd((rows, hid), bf),
+        ),
+        in_specs=[vm, vm, vm, vm, hbm, hbm],
+        out_specs=(vm,) * 6,
+        scratch_shapes=[
+            V(blocks, tok, 2 * feat + LANES), V(feat, hid), V(hid, feat), V(rows, feat),
+            pltpu.VMEM((rows, LANES), jnp.float32),
+            V(zs, 2, 2, 2, tok, width), V(zs, 2, 2, tok, width), V(zs, 2, 2, tok, width),
+            V(zs, 2, tok, width), V(zs, 2, tok, width), V(zs, tok, width),
+            V(zs, tok, width), V(zs - 1, tok, width),
+            dma(2), dma(zs), dma(zs), dma(zs), dma(zs), dma(zs), dma(zs),
+            dma(zs), dma(zs), dma(zs), dma(zs), dma(4 * zs), dma(4 * zs),
+            dma(nc), dma(nc), dma(nc), dma(nc), dma(nc), dma(nc), dma(nc * zs), dma(nc * zs),
+        ],
+        compiler_params=pltpu.CompilerParams(
+            collective_id=0, has_side_effects=True, vmem_limit_bytes=48 << 20),
+        cost_estimate=pl.CostEstimate(
+            flops=6 * rows * feat * hid, bytes_accessed=4 * feat * hid, transcendentals=0),
+    )(tokens, cotangent, expert_ids.T, gates.T, w_in[0], w_out[0])
+    dims = (((0,), (0,)), ((), ()))
+    g1 = lax.dot_general(xr, pg, dims, preferred_element_type=jnp.float32).astype(bf)
+    g2 = lax.dot_general(hd, sc, dims, preferred_element_type=jnp.float32).astype(bf)
+    return grads, gate.T, g1[None], g2[None]
 
 
 def normal_parts(pre):
@@ -114,6 +424,19 @@
         P("expert", None, "dp"),
         P("expert", "dp", None),
     )
-    return jax.shard_map(
-        per_device, mesh=mesh, in_specs=in_specs, out_specs=out_specs, check_vma=False
-    )
+    sizes = dict(mesh.shape)
+
+    def run(tokens, *rest):
+        zs = sizes["dp"]
+        row_bytes = 2 * (2 * tokens.shape[1] + LANES)
+        small = tokens.shape[0] * row_bytes <= GATHER_BYTES
+        cube = sizes["expert"] == 8 and zs > 1 and zs & (zs - 1) == 0
+        plan = fused if small and cube else per_device
+        return mapped(plan)(tokens, *rest)
+
+    def mapped(plan):
+        return jax.shard_map(
+            plan, mesh=mesh, in_specs=in_specs, out_specs=out_specs, check_vma=False
+        )
+
+    return run

time: 136 us -> 60.3 us (0.44)
  blocking collectives: 60.6 us -> 0 us
  Pallas kernels: 0 us -> 49.5 us
  starting transfers between devices: 21.4 us -> 0 us
  matrix products: 20.1 us -> 5.75 us
  between operations: 14.8 us -> 0.65 us
  waiting for transfers between devices: 7.34 us -> 0 us
  local copies, waits for them, and re-layouts: 10.7 us -> 4.07 us
    all_gather x3 -> x0, blocking collectives: 50.8 us -> none  [the longest x1 19.5 us: per_device(): cot_blocks = lax.all_gather(arrived[1], 'dp', axis=0, tiled=True)]
    pallas_call x0 -> x1, Pallas kernels: none -> 49.5 us  [fused(): pl.pallas_call(functools.partial(fused_kernel, tok, feat, hid, zs, cap, t...]
    all_to_all x5 -> x0, starting transfers between devices: 21.4 us -> none  [the longest x1 5.17 us: per_device(): lax.all_to_all(send_gate, 'expert', split_axis=0, concat_axis=0, tiled=True)]
    dot_general x11 -> x2, matrix products: 20.1 us -> 5.75 us  [the longest x1 2.92 us: fused(): lax.dot_general(hd, sc, dims, preferred_element_type=jnp.float32).astype(bf)]
    unnamed x1 -> x0, blocking collectives: 9.82 us -> none
    all_to_all x5 -> x0, waiting for transfers between devices: 7.01 us -> none  [the longest x1 5.74 us: per_device(): lax.all_to_all(row_back, 'expert', split_axis=0, concat_axis=0, tiled=True)]
    broadcast_in_dim x2 -> x0, local copies, waits for them, and re-layouts: 3.02 us -> none  [the longest x1 1.51 us: per_device(): src_cot = jnp.repeat(cotangent, 2, axis=0)]
    reshape x4 -> x0, local copies, waits for them, and re-layouts: 2.06 us -> none  [the longest x1 0.94 us: per_device(): src_in = jnp.repeat(tokens, 2, axis=0)]
  transfers between devices with their start and end apart: 6 -> 0, of which waited for: 3 -> 0; matrix products, arithmetic and copies ran while one was open for 13% -> 0% of each run, Pallas kernels for 0% -> 0%
where the time goes in v2:
time: 60.3 us; the launch traced here: 60 us
  Pallas kernels  49.5 us (82%)
  matrix products  5.75 us (10%)
  local copies, waits for them, and re-layouts  4.07 us (7%)
  between operations  0.65 us (1%)
    pallas_call x1, Pallas kernels, fused(): pl.pallas_call(functools.partial(fused_kernel, tok, feat, hid, zs, cap, t...  49.5 us
    unnamed x10, local copies, waits for them, and re-layouts  4.07 us
    dot_general x1, matrix products, fused(): lax.dot_general(hd, sc, dims, preferred_element_type=jnp.float32).astype(bf)  2.92 us
    dot_general x1, matrix products, fused(): lax.dot_general(xr, pg, dims, preferred_element_type=jnp.float32).astype(bf)  2.83 us

profile of v2, /device:TPU:0, one launch (start us, length us, event | category | flops | bytes accessed | tf_op | source)
XLA Modules:
  0.0 60.0 jit_solution(8750559163607179550)
XLA Ops:
  0.6 0.0 copy-start
  0.6 0.8 %copy-done = bf16[16,1664]{1,0:T(8,128)(2,1)S(1)} copy-done((bf16[16,1664]{1,0:T(8,128)(2,1)S(1)}, bf16[16,1664]{1,0:T(8,128)(2,1)}, u32[]{:S(2)}) %copy-start) | copy-done | bytes 53272
  1.4 0.0 copy-start.1
  1.4 0.8 %copy-done.1 = bf16[16,1664]{1,0:T(8,128)(2,1)S(1)} copy-done((bf16[16,1664]{1,0:T(8,128)(2,1)S(1)}, bf16[16,1664]{1,0:T(8,128)(2,1)}, u32[]{:S(2)}) %copy-start.1) | copy-done | bytes 53272
  2.3 0.0 copy-start.2
  2.3 0.7 %copy-done.2 = s32[16,2]{0,1:T(2,128)S(1)} copy-done((s32[16,2]{0,1:T(2,128)S(1)}, s32[16,2]{0,1:T(2,128)}, u32[]{:S(2)}) %copy-start.2) | copy-done | bytes 152
  2.9 0.0 copy-start.3
  2.9 0.7 %copy-done.3 = bf16[16,2]{0,1:T(2,128)(2,1)S(1)} copy-done((bf16[16,2]{0,1:T(2,128)(2,1)S(1)}, bf16[16,2]{0,1:T(2,128)(2,1)}, u32[]{:S(2)}) %copy-start.3) | copy-done | bytes 88
  3.6 49.5 %shard_map.93 = (bf16[16,1664]{1,0:T(8,128)(2,1)S(1)}, bf16[2,16]{1,0:T(2,128)(2,1)S(1)}, bf16[256,1664]{1,0:T(8,128)(2,1)S(1)}, bf16[256,1664]{1,0:T(8,128)(2,1...) custom-call(bf16[16,1664]{1,0:T(8,128)(2,1)S(1)} %copy-done, bf16[16,1664]{1,0:T(8,128)(2,1)S(1)} %copy-done.1, ...), custom_call_target="tpu_custom_call" | custom-call | flops 2617245696 | bytes 6815744 | tf_op jit(solution)/shard_map/pallas_call | solution.py:288
  53.1 2.8 %fusion = bf16[1,1664,1024]{2,1,0:T(8,128)(2,1)} fusion(bf16[256,1664]{1,0:T(8,128)(2,1)S(1)} %get-tuple-element.12, bf16[256,1024]{1,0:T(8,128)(2,1)S(1)} %get-tuple-element.13), kind=kOutput, calls=%fused_computation.2 | convolution fusion | flops 874119168 | bytes 4784128 | tf_op jit(solution)/shard_map/dot_general | solution.py:312
  56.0 2.9 %fusion.1 = bf16[1,1024,1664]{2,1,0:T(8,128)(2,1)} fusion(bf16[256,1024]{1,0:T(8,128)(2,1)S(1)} %get-tuple-element.14, bf16[256,1664]{1,0:T(8,128)(2,1)S(1)} %get-tuple-element.15), kind=kOutput, calls=%fused_computation.3 | convolution fusion | flops 874119168 | bytes 4784128 | tf_op jit(solution)/shard_map/dot_general | solution.py:313
  58.9 0.6 %copy.12 = bf16[16,1664]{1,0:T(8,128)(2,1)} copy(bf16[16,1664]{1,0:T(8,128)(2,1)S(1)} %get-tuple-element.20) | data formatting | bytes 106496
  59.5 0.5 copy.13
Async XLA Ops:
  0.6 0.8 %copy-start = (bf16[16,1664]{1,0:T(8,128)(2,1)S(1)}, bf16[16,1664]{1,0:T(8,128)(2,1)}, u32[]{:S(2)}) copy-start(bf16[16,1664]{1,0:T(8,128)(2,1)} %tok_ref.1) | copy-start | bytes 159748
  1.4 0.8 %copy-start.1 = (bf16[16,1664]{1,0:T(8,128)(2,1)S(1)}, bf16[16,1664]{1,0:T(8,128)(2,1)}, u32[]{:S(2)}) copy-start(bf16[16,1664]{1,0:T(8,128)(2,1)} %cot_ref.1) | copy-start | bytes 159748
  2.3 0.7 %copy-start.2 = (s32[16,2]{0,1:T(2,128)S(1)}, s32[16,2]{0,1:T(2,128)}, u32[]{:S(2)}) copy-start(s32[16,2]{0,1:T(2,128)} %param.8) | copy-start | bytes 388
  2.9 0.7 %copy-start.3 = (bf16[16,2]{0,1:T(2,128)(2,1)S(1)}, bf16[16,2]{0,1:T(2,128)(2,1)}, u32[]{:S(2)}) copy-start(bf16[16,2]{0,1:T(2,128)(2,1)} %param.9) | copy-start | bytes 196

commit v3 on v2

--- a/solution.py
+++ b/solution.py
@@ -141,8 +141,8 @@
         CR[sl, :] = cr.astype(bf)
         sc_ref[sl, :] = (gate[:, 0:1] * cr).astype(bf)
 
-    def hidden_step(g, i):
-        sl, fs = slice(g * gr, (g + 1) * gr), slice(i * step, (i + 1) * step)
+    def hidden_step(i):
+        sl, fs = slice(0, 2 * gr), slice(i * step, (i + 1) * step)
         pre = jnp.dot(xr_ref[sl, :], W1[:, fs], preferred_element_type=f32)
         back = lax.dot_general(CR[sl, :], W2[fs, :], ndims, preferred_element_type=f32)
         cdf = 0.5 * (1.0 + lax.erf(pre * 0.7071067811865476))
@@ -151,7 +151,9 @@
         hid_ref[sl, fs] = h
         pg_ref[sl, fs] = (BE[sl, 0:1] * back * (cdf + pre * pdf)).astype(bf)
         t = jnp.sum(h.astype(f32) * back, axis=1, keepdims=True)
-        gsums[g] = t if gsums[g] is None else gsums[g] + t
+        for g in range(2):
+            part = t[g * gr:(g + 1) * gr]
+            gsums[g] = part if gsums[g] is None else gsums[g] + part
 
     for d in range(1, zs):
         zc.append(go(G.at[blk(e, 0)], G.at[blk(e, d)], zs_s.at[d], zs_r.at[d], (e, zp[d])))
@@ -163,21 +165,15 @@
             diag(j - 1)
     for j in range(zh):
         finish(j)
-    steps = hid // step
+    diag(zs - 1)
+    for j in range(zh, zs):
+        finish(j)
     pick_group(0)
+    pick_group(1)
     for l in loads:
         l.wait()
-    for i in range(steps // 2):
-        hidden_step(0, i)
-    diag(zs - 1)
-    for j in range(zh, zs - 1):
-        finish(j)
-    for i in range(steps // 2, steps):
-        hidden_step(0, i)
-    finish(zs - 1)
-    pick_group(1)
-    for i in range(steps):
-        hidden_step(1, i)
+    for i in range(hid // step):
+        hidden_step(i)
 
     def place(i):
         lo, w = chunks[i]

time: 60.3 us -> 59.7 us (0.990)
  no operation moved by 1% of the time
where the time goes in v3:
time: 59.7 us; the launch traced here: 59.4 us
  Pallas kernels  49 us (82%)
  matrix products  5.75 us (10%)
  local copies, waits for them, and re-layouts  4.07 us (7%)
  between operations  0.65 us (1%)
    pallas_call x1, Pallas kernels, fused(): pl.pallas_call(functools.partial(fused_kernel, tok, feat, hid, zs, cap, t...  49 us
    unnamed x10, local copies, waits for them, and re-layouts  4.07 us
    dot_general x1, matrix products, fused(): lax.dot_general(hd, sc, dims, preferred_element_type=jnp.float32).astype(bf)  2.92 us
    dot_general x1, matrix products, fused(): lax.dot_general(xr, pg, dims, preferred_element_type=jnp.float32).astype(bf)  2.83 us

profile of v3, /device:TPU:0, one launch (start us, length us, event | category | flops | bytes accessed | tf_op | source)
XLA Modules:
  0.0 59.4 jit_solution(7691861276331906923)
XLA Ops:
  0.6 0.0 copy-start
  0.6 0.8 %copy-done = bf16[16,1664]{1,0:T(8,128)(2,1)S(1)} copy-done((bf16[16,1664]{1,0:T(8,128)(2,1)S(1)}, bf16[16,1664]{1,0:T(8,128)(2,1)}, u32[]{:S(2)}) %copy-start) | copy-done | bytes 53272
  1.4 0.0 copy-start.1
  1.4 0.8 %copy-done.1 = bf16[16,1664]{1,0:T(8,128)(2,1)S(1)} copy-done((bf16[16,1664]{1,0:T(8,128)(2,1)S(1)}, bf16[16,1664]{1,0:T(8,128)(2,1)}, u32[]{:S(2)}) %copy-start.1) | copy-done | bytes 53272
  2.3 0.0 copy-start.2
  2.3 0.7 %copy-done.2 = s32[16,2]{0,1:T(2,128)S(1)} copy-done((s32[16,2]{0,1:T(2,128)S(1)}, s32[16,2]{0,1:T(2,128)}, u32[]{:S(2)}) %copy-start.2) | copy-done | bytes 152
  2.9 0.0 copy-start.3
  2.9 0.7 %copy-done.3 = bf16[16,2]{0,1:T(2,128)(2,1)S(1)} copy-done((bf16[16,2]{0,1:T(2,128)(2,1)S(1)}, bf16[16,2]{0,1:T(2,128)(2,1)}, u32[]{:S(2)}) %copy-start.3) | copy-done | bytes 88
  3.6 49.0 %shard_map.93 = (bf16[16,1664]{1,0:T(8,128)(2,1)S(1)}, bf16[2,16]{1,0:T(2,128)(2,1)S(1)}, bf16[256,1664]{1,0:T(8,128)(2,1)S(1)}, bf16[256,1664]{1,0:T(8,128)(2,1...) custom-call(bf16[16,1664]{1,0:T(8,128)(2,1)S(1)} %copy-done, bf16[16,1664]{1,0:T(8,128)(2,1)S(1)} %copy-done.1, ...), custom_call_target="tpu_custom_call" | custom-call | flops 2617245696 | bytes 6815744 | tf_op jit(solution)/shard_map/pallas_call | solution.py:284
  52.6 2.8 %fusion = bf16[1,1664,1024]{2,1,0:T(8,128)(2,1)} fusion(bf16[256,1664]{1,0:T(8,128)(2,1)S(1)} %get-tuple-element.12, bf16[256,1024]{1,0:T(8,128)(2,1)S(1)} %get-tuple-element.13), kind=kOutput, calls=%fused_computation.2 | convolution fusion | flops 874119168 | bytes 4784128 | tf_op jit(solution)/shard_map/dot_general | solution.py:308
  55.4 2.9 %fusion.1 = bf16[1,1024,1664]{2,1,0:T(8,128)(2,1)} fusion(bf16[256,1024]{1,0:T(8,128)(2,1)S(1)} %get-tuple-element.14, bf16[256,1664]{1,0:T(8,128)(2,1)S(1)} %get-tuple-element.15), kind=kOutput, calls=%fused_computation.3 | convolution fusion | flops 874119168 | bytes 4784128 | tf_op jit(solution)/shard_map/dot_general | solution.py:309
  58.3 0.6 %copy.12 = bf16[16,1664]{1,0:T(8,128)(2,1)} copy(bf16[16,1664]{1,0:T(8,128)(2,1)S(1)} %get-tuple-element.20) | data formatting | bytes 106496
  58.9 0.5 copy.13
Async XLA Ops:
  0.6 0.8 %copy-start = (bf16[16,1664]{1,0:T(8,128)(2,1)S(1)}, bf16[16,1664]{1,0:T(8,128)(2,1)}, u32[]{:S(2)}) copy-start(bf16[16,1664]{1,0:T(8,128)(2,1)} %tok_ref.1) | copy-start | bytes 159748
  1.4 0.8 %copy-start.1 = (bf16[16,1664]{1,0:T(8,128)(2,1)S(1)}, bf16[16,1664]{1,0:T(8,128)(2,1)}, u32[]{:S(2)}) copy-start(bf16[16,1664]{1,0:T(8,128)(2,1)} %cot_ref.1) | copy-start | bytes 159748
  2.3 0.7 %copy-start.2 = (s32[16,2]{0,1:T(2,128)S(1)}, s32[16,2]{0,1:T(2,128)}, u32[]{:S(2)}) copy-start(s32[16,2]{0,1:T(2,128)} %param.8) | copy-start | bytes 388
  2.9 0.7 %copy-start.3 = (bf16[16,2]{0,1:T(2,128)(2,1)S(1)}, bf16[16,2]{0,1:T(2,128)(2,1)}, u32[]{:S(2)}) copy-start(bf16[16,2]{0,1:T(2,128)(2,1)} %param.9) | copy-start | bytes 196
